TPU v7x, 32 devices: a whole 2x2x4 slice. The times are simulated.
32 devices in a mesh: parts: 2 (over y), warp: 4 (over z), weft: 2 (over x), ply: 2 (over core).
Axes of the slice: x: 2, y: 2, z: 4, core: 2. Of those that a mesh axis runs over, the one named last changes fastest.
Arguments:
- lam_start: float32 [64, 256, 512], P(('parts', 'warp', 'ply'), 'weft'), parts along dimension 0, as said below
- resid_start: float32 [64, 256, 512], P(('parts', 'warp', 'ply'), 'weft'), parts along dimension 0, as said below
- dirn_start: float32 [64, 256, 512], P(('parts', 'warp', 'ply'), 'weft'), parts along dimension 0, as said below
- rz_start: float32 [2], P('parts'), parts along dimension 0, may hold values from 10485760 to 83886080
- pattern: int32 [64, 256], P(('parts', 'warp', 'ply'), 'weft'), parts along dimension 0, may hold values from 0 to 2
- corners: int32 [4, 64, 256], P(None, ('parts', 'warp', 'ply'), 'weft'), parts along dimension 1, may hold values from -1 to 127, as said below
- schur_inv: float32 [3, 512, 512], replicated, as said below
- schur_dirichlet: float32 [3, 512, 512], replicated, as said below
- corner_shape: float32 [3, 4, 512], replicated, may hold values from -0.3 to 0.3
- coarse_inv: float32 [256, 128], P(('parts', 'warp', 'weft', 'ply')), parts along dimension 0, as said below
Outputs:
- lam_final: float32 [64, 256, 512], P(('parts', 'warp', 'ply'), 'weft'), parts along dimension 0
- resid_final: float32 [64, 256, 512], P(('parts', 'warp', 'ply'), 'weft'), parts along dimension 0
- dirn_final: float32 [64, 256, 512], P(('parts', 'warp', 'ply'), 'weft'), parts along dimension 0
There are 2 independent parts, one for each index of `parts`. A program takes and returns all parts, laid end to end along the dimension named above; an argument that names none is the same for every part. Nothing has to cross between parts.
Inputs may be any that keep to these rules, and one draw needn't show every extreme that they name: `lam_start`: in each cell the W block is minus the E block of the cell to its west and zero where j = 0; the S block is minus the N block of the cell to its south and zero where i = 0. `resid_start`: in each cell the W block is minus the E block of the cell to its west and zero where j = 0; the S block is minus the N block of the cell to its south and zero where i = 0. `dirn_start`: in each cell the W block is minus the E block of the cell to its west and zero where j = 0; the S block is minus the N block of the cell to its south and zero where i = 0. `corners`: corner k of cell (i, j) is the corner node (i, j), (i, j + 1), (i + 1, j) or (i + 1, j + 1) for k = 0, 1, 2, 3; nodes (a, b) with a = 32 or b = 256 are -1; every other node's row is that of its aggregate, the block of 8 x 8 nodes with the same a // 8 and b // 8; each aggregate has its own row, and which aggregate has which row is drawn. `schur_inv`: each matrix is symmetric positive definite. `schur_dirichlet`: each matrix is symmetric positive definite. `coarse_inv`: symmetric positive definite.
All inputs are finite; a program needn't handle non-finite values.
Results may differ from a plain program's by a relative error of at most 0.00027.
Values sent between devices are 32-bit elements; how exact they have to be, the bound alone decides.
A program may use at most 64 MiB of HBM per device.

v0:
```python
import jax
import jax.numpy as jnp
from jax import lax
from jax.sharding import PartitionSpec as P

ITERS = 3
HIGHEST = lax.Precision.HIGHEST


def with_halo(array, sides, width):
    for axis, dim in sides:
        count, length = (lax.axis_size(axis), array.shape[dim])
        up = [(i, (i + 1) % count) for i in range(count - 1)]
        down = [(j, i) for i, j in up]
        last = lax.slice_in_dim(array, length - width, length, axis=dim)
        leading = lax.slice_in_dim(array, 0, width, axis=dim)
        before = lax.ppermute(last, axis, up)
        after = lax.ppermute(leading, axis, down)
        array = jnp.concatenate([before, array, after], axis=dim)
    return array


def split_edges(values, edge_len):
    return (
        values[..., :edge_len],
        values[..., edge_len : 2 * edge_len],
        values[..., 2 * edge_len : 3 * edge_len],
        values[..., 3 * edge_len :],
    )


def cross_faces(values, edge_len, west_keep, south_keep):
    west_side, east_side, south_side, north_side = split_edges(values, edge_len)
    rows_here, cols_here = (values.shape[0], values.shape[1])
    local_row = lax.broadcasted_iota(jnp.int32, (rows_here, cols_here, 1), 0)
    local_col = lax.broadcasted_iota(jnp.int32, (rows_here, cols_here, 1), 1)
    along_rows = jnp.where(local_row == 0, south_side, north_side)
    along_cols = jnp.where(local_col == 0, west_side, east_side)
    padded = with_halo(
        jnp.concatenate([along_rows, along_cols], axis=2), ((("warp", "ply"), 0), ("weft", 1)), 1
    )
    from_south = padded[0, 1:-1, :edge_len]
    from_north = padded[-1, 1:-1, :edge_len]
    from_west = padded[1:-1, 0, edge_len:]
    from_east = padded[1:-1, -1, edge_len:]
    east_west = jnp.concatenate([west_side[:, 1:], from_east[:, None]], axis=1)
    west_east = jnp.concatenate([from_west[:, None], east_side[:, :-1]], axis=1)
    north_south = jnp.concatenate([south_side[1:], from_north[None]], axis=0)
    south_north = jnp.concatenate([from_south[None], north_side[:-1]], axis=0)
    return jnp.concatenate(
        [
            (west_side - west_east) * west_keep,
            east_side - east_west,
            (south_side - south_north) * south_keep,
            north_side - north_south,
        ],
        axis=2,
    )


def apply_cells(rows_flat, matrices, cell_order, inverse, group_sizes):
    sorted_rows = rows_flat[cell_order]
    product = lax.ragged_dot(
        sorted_rows, matrices, group_sizes, precision=HIGHEST, preferred_element_type=jnp.float32
    )
    return product[inverse]


def on_device(
    lam_start,
    resid_start,
    dirn_start,
    rz_start,
    pattern,
    corners,
    schur_inv,
    schur_dirichlet,
    corner_shape,
    coarse_inv,
):
    rows_here, cols_here, dof_count = lam_start.shape
    edge_len = dof_count // 4
    pattern_count = schur_inv.shape[0]
    coarse_count = coarse_inv.shape[1]
    row_pos = (
        lax.broadcasted_iota(jnp.int32, (rows_here, cols_here, 1), 0)
        + lax.axis_index(("warp", "ply")) * rows_here
    )
    col_pos = (
        lax.broadcasted_iota(jnp.int32, (rows_here, cols_here, 1), 1)
        + lax.axis_index("weft") * cols_here
    )
    total_rows = lax.axis_size(("warp", "ply")) * rows_here
    total_cols = lax.axis_size("weft") * cols_here
    west_keep = (col_pos > 0).astype(jnp.float32)
    south_keep = (row_pos > 0).astype(jnp.float32)
    east_weight = jnp.where(col_pos == total_cols - 1, 1.0, 0.5).astype(jnp.float32)
    north_weight = jnp.where(row_pos == total_rows - 1, 1.0, 0.5).astype(jnp.float32)
    block_shape = (rows_here, cols_here, edge_len)
    edge_weight = jnp.concatenate(
        [
            jnp.broadcast_to(0.5 * west_keep, block_shape),
            jnp.broadcast_to(east_weight, block_shape),
            jnp.broadcast_to(0.5 * south_keep, block_shape),
            jnp.broadcast_to(north_weight, block_shape),
        ],
        axis=2,
    )
    cell_kind = pattern.reshape(-1)
    cell_order = jnp.argsort(cell_kind, stable=True)
    inverse = jnp.argsort(cell_order, stable=True)
    selector = (cell_kind[None, :] == jnp.arange(pattern_count, dtype=jnp.int32)[:, None]).astype(
        jnp.float32
    )
    group_sizes = jnp.sum(selector, axis=1).astype(jnp.int32)
    corner_rows = corners.reshape(4, -1)
    corner_live = corner_rows >= 0
    corner_slot = jnp.where(corner_live, corner_rows, coarse_count)
    corner_pick = jnp.where(corner_live, corner_rows, 0)
    multiplier, residual, direction = (lam_start, resid_start, dirn_start)
    rz_prev = rz_start[0]
    for iteration in range(ITERS):
        scaled = (edge_weight * residual).reshape(-1, dof_count)
        spread = apply_cells(scaled, schur_dirichlet, cell_order, inverse, group_sizes).reshape(
            residual.shape
        )
        precond = edge_weight * cross_faces(spread, edge_len, west_keep, south_keep)
        rz_now = lax.psum(jnp.sum(edge_weight * residual * precond), ("warp", "weft", "ply"))
        direction = precond + rz_now / rz_prev * direction
        rows_flat = direction.reshape(-1, dof_count)
        local_image = apply_cells(rows_flat, schur_inv, cell_order, inverse, group_sizes)
        corner_terms = jnp.einsum("pkd,cd->pkc", corner_shape, rows_flat, precision=HIGHEST)
        corner_load = jnp.sum(corner_terms * selector[:, None, :], axis=0)
        partial_rhs = jax.ops.segment_sum(
            corner_load.reshape(-1), corner_slot.reshape(-1), num_segments=coarse_count + 1
        )[:coarse_count]
        coarse_rhs = lax.psum(partial_rhs, ("warp", "weft", "ply"))
        coarse_sol = lax.all_gather(
            jnp.dot(coarse_inv, coarse_rhs, precision=HIGHEST),
            ("warp", "weft", "ply"),
            axis=0,
            tiled=True,
        )
        corner_vals = jnp.where(corner_live, coarse_sol[corner_pick], 0.0)
        full_image = local_image + jnp.einsum(
            "pkc,pkd->cd", selector[:, None, :] * corner_vals[None], corner_shape, precision=HIGHEST
        )
        applied = cross_faces(full_image.reshape(direction.shape), edge_len, west_keep, south_keep)
        curvature = lax.psum(jnp.sum(edge_weight * direction * applied), ("warp", "weft", "ply"))
        alpha_step = rz_now / curvature
        multiplier = multiplier + alpha_step * direction
        residual = residual - alpha_step * applied
        rz_prev = rz_now
    return (multiplier, residual, direction)


def solution(mesh):
    return jax.shard_map(
        on_device,
        mesh=mesh,
        in_specs=(
            P(("parts", "warp", "ply"), "weft", None),
            P(("parts", "warp", "ply"), "weft", None),
            P(("parts", "warp", "ply"), "weft", None),
            P("parts"),
            P(("parts", "warp", "ply"), "weft"),
            P(None, ("parts", "warp", "ply"), "weft"),
            P(),
            P(),
            P(),
            P(("parts", "warp", "weft", "ply"), None),
        ),
        out_specs=(
            P(("parts", "warp", "ply"), "weft", None),
            P(("parts", "warp", "ply"), "weft", None),
            P(("parts", "warp", "ply"), "weft", None),
        ),
        check_vma=False,
    )
```

profile of v0, /device:TPU:0, one launch (start us, length us, event | category | flops | bytes accessed | tf_op | source)
XLA Modules:
  0.0 678.7 jit_solution(7160559662432840204)
XLA Ops:
  15.8 8.7 %ragged-dot-none.5 = f32[512,512]{1,0:T(8,128)} custom-call(s32[1]{0:T(128)} %get-tuple-element.27, s32[4]{0:T(128)} %get-tuple-element.28, s32[4]{0:T(128)} %get-tuple-element.29, s32[4]{0:T(128)} %get-tuple-element.30, s32[1]{0:T(128)} %get-tuple-element.27, f32[512,512]{1,0:T(8,128)} %gather_fusion, f32[3,512,512]{2,1,0:T(8,128)} %param.17), custom_call_target="tpu_custom_call" | custom-call | flops 268435456 | bytes 5242892 | tf_op jit(solution)/shard_map/ragged_dot_general/ragged-dot-none
  50.5 33.6 %psum.63 = f32[]{:T(128)} all-reduce(f32[]{:T(128)} %multiply_reduce_fusion.2), channel_id=1, replica_groups=mesh['parts'=2,'warp'=4,'weft'=2,'ply'=2] {'warp','weft','ply'}, use_global_device_ids=true, to_apply=%region_4.5 | all-reduce | flops 1 | bytes 8 | tf_op jit(solution)/shard_map/psum | solution.py:128
  87.2 14.7 %scatter_custom_fusion = f32[129]{0:T(256)S(1)} fusion(s32[2048]{0:T(1024)S(1)} %bitcast.138, f32[2048]{0:T(1024)S(1)} %bitcast.142, f32[]{:T(128)} %constant.17.clone.1), kind=kCustom, calls=%fused_computation.187 | custom fusion | flops 2048 | bytes 520 | tf_op jit(solution)/shard_map/scatter-add | solution.py:134
  101.8 29.5 %psum.64 = f32[128]{0:T(128)S(1)} all-reduce(f32[128]{0:T(128)S(1)} %slice.337), channel_id=1, replica_groups=mesh['parts'=2,'warp'=4,'weft'=2,'ply'=2] {'warp','weft','ply'}, use_global_device_ids=true, to_apply=%region_7.8 | all-reduce | flops 128 | bytes 1024 | tf_op jit(solution)/shard_map/psum | solution.py:137
  131.7 29.5 %all-reduce = f32[128]{0:T(128)S(1)} all-reduce(f32[128]{0:T(128)S(1)} %dynamic-update-slice), channel_id=1, replica_groups=mesh['parts'=2,'warp'=4,'weft'=2,'ply'=2] {'warp','weft','ply'}, use_global_device_ids=true, to_apply=%add | all-reduce | flops 128 | bytes 1024
  161.1 12.6 %gather_fusion.4 = f32[2048]{0:T(1024)S(1)} fusion(f32[128]{0:T(128)S(1)} %all-reduce, s32[2048]{0:T(1024)S(1)} %broadcast_clamp_fusion), kind=kCustom, calls=%fused_computation.4 | custom fusion | bytes 24576 | tf_op jit(solution)/shard_map/gather | solution.py:144
  176.1 8.7 %ragged-dot-none.4 = f32[512,512]{1,0:T(8,128)} custom-call(s32[1]{0:T(128)} %get-tuple-element.27, s32[4]{0:T(128)} %get-tuple-element.28, s32[4]{0:T(128)} %get-tuple-element.29, s32[4]{0:T(128)} %get-tuple-element.30, s32[1]{0:T(128)} %get-tuple-element.27, f32[512,512]{1,0:T(8,128)} %gather_fusion.2, f32[3,512,512]{2,1,0:T(8,128)} %param.16), custom_call_target="tpu_custom_call" | custom-call | flops 268435456 | bytes 5242892 | tf_op jit(solution)/shard_map/ragged_dot_general/ragged-dot-none
  205.1 32.0 %psum.65 = f32[]{:T(128)} all-reduce(f32[]{:T(128)} %fusion.23), channel_id=1, replica_groups=mesh['parts'=2,'warp'=4,'weft'=2,'ply'=2] {'warp','weft','ply'}, use_global_device_ids=true, to_apply=%region_9.10 | all-reduce | flops 1 | bytes 8 | tf_op jit(solution)/shard_map/psum | solution.py:149
  242.4 8.7 %ragged-dot-none.3 = f32[512,512]{1,0:T(8,128)} custom-call(s32[1]{0:T(128)} %get-tuple-element.27, s32[4]{0:T(128)} %get-tuple-element.28, s32[4]{0:T(128)} %get-tuple-element.29, s32[4]{0:T(128)} %get-tuple-element.30, s32[1]{0:T(128)} %get-tuple-element.27, f32[512,512]{1,0:T(8,128)} %gather_fusion.5, f32[3,512,512]{2,1,0:T(8,128)} %param.17), custom_call_target="tpu_custom_call" | custom-call | flops 268435456 | bytes 5242892 | tf_op jit(solution)/shard_map/ragged_dot_general/ragged-dot-none
  270.0 30.6 %psum.66 = f32[]{:T(128)} all-reduce(f32[]{:T(128)} %multiply_reduce_fusion.1), channel_id=1, replica_groups=mesh['parts'=2,'warp'=4,'weft'=2,'ply'=2] {'warp','weft','ply'}, use_global_device_ids=true, to_apply=%region_11.12 | all-reduce | flops 1 | bytes 8 | tf_op jit(solution)/shard_map/psum | solution.py:128
  304.3 14.7 %scatter_custom_fusion.1 = f32[129]{0:T(256)S(1)} fusion(s32[2048]{0:T(1024)S(1)} %bitcast.139, f32[2048]{0:T(1024)S(1)} %bitcast.143, f32[]{:T(128)} %constant.17.clone.1), kind=kCustom, calls=%fused_computation.185 | custom fusion | flops 2048 | bytes 520 | tf_op jit(solution)/shard_map/scatter-add | solution.py:134
  319.0 29.5 %psum.67 = f32[128]{0:T(128)S(1)} all-reduce(f32[128]{0:T(128)S(1)} %slice.370), channel_id=1, replica_groups=mesh['parts'=2,'warp'=4,'weft'=2,'ply'=2] {'warp','weft','ply'}, use_global_device_ids=true, to_apply=%region_14.15 | all-reduce | flops 128 | bytes 1024 | tf_op jit(solution)/shard_map/psum | solution.py:137
  348.8 29.5 %all-reduce.1 = f32[128]{0:T(128)S(1)} all-reduce(f32[128]{0:T(128)S(1)} %dynamic-update-slice.1), channel_id=1, replica_groups=mesh['parts'=2,'warp'=4,'weft'=2,'ply'=2] {'warp','weft','ply'}, use_global_device_ids=true, to_apply=%add.1 | all-reduce | flops 128 | bytes 1024
  378.3 12.6 %gather_fusion.9 = f32[2048]{0:T(1024)S(1)} fusion(f32[128]{0:T(128)S(1)} %all-reduce.1, s32[2048]{0:T(1024)S(1)} %broadcast_clamp_fusion), kind=kCustom, calls=%fused_computation.9 | custom fusion | bytes 24576 | tf_op jit(solution)/shard_map/gather | solution.py:144
  393.3 8.7 %ragged-dot-none.2 = f32[512,512]{1,0:T(8,128)} custom-call(s32[1]{0:T(128)} %get-tuple-element.27, s32[4]{0:T(128)} %get-tuple-element.28, s32[4]{0:T(128)} %get-tuple-element.29, s32[4]{0:T(128)} %get-tuple-element.30, s32[1]{0:T(128)} %get-tuple-element.27, f32[512,512]{1,0:T(8,128)} %gather_fusion.7, f32[3,512,512]{2,1,0:T(8,128)} %param.16), custom_call_target="tpu_custom_call" | custom-call | flops 268435456 | bytes 5242892 | tf_op jit(solution)/shard_map/ragged_dot_general/ragged-dot-none
  422.3 32.2 %psum.68 = f32[]{:T(128)} all-reduce(f32[]{:T(128)} %fusion.22), channel_id=1, replica_groups=mesh['parts'=2,'warp'=4,'weft'=2,'ply'=2] {'warp','weft','ply'}, use_global_device_ids=true, to_apply=%region_16.17 | all-reduce | flops 1 | bytes 8 | tf_op jit(solution)/shard_map/psum | solution.py:149
  461.6 8.7 %ragged-dot-none.1 = f32[512,512]{1,0:T(8,128)} custom-call(s32[1]{0:T(128)} %get-tuple-element.27, s32[4]{0:T(128)} %get-tuple-element.28, s32[4]{0:T(128)} %get-tuple-element.29, s32[4]{0:T(128)} %get-tuple-element.30, s32[1]{0:T(128)} %get-tuple-element.27, f32[512,512]{1,0:T(8,128)} %gather_fusion.10, f32[3,512,512]{2,1,0:T(8,128)} %param.17), custom_call_target="tpu_custom_call" | custom-call | flops 268435456 | bytes 5242892 | tf_op jit(solution)/shard_map/ragged_dot_general/ragged-dot-none
  488.3 30.6 %psum.69 = f32[]{:T(128)} all-reduce(f32[]{:T(128)} %multiply_reduce_fusion), channel_id=1, replica_groups=mesh['parts'=2,'warp'=4,'weft'=2,'ply'=2] {'warp','weft','ply'}, use_global_device_ids=true, to_apply=%region_18.19 | all-reduce | flops 1 | bytes 8 | tf_op jit(solution)/shard_map/psum | solution.py:128
  522.9 14.7 %scatter_custom_fusion.2 = f32[129]{0:T(256)S(1)} fusion(s32[2048]{0:T(1024)S(1)} %bitcast.140, f32[2048]{0:T(1024)S(1)} %bitcast.141, f32[]{:T(128)} %constant.17.clone.1), kind=kCustom, calls=%fused_computation.183 | custom fusion | flops 2048 | bytes 520 | tf_op jit(solution)/shard_map/scatter-add | solution.py:134
  537.5 29.5 %psum.70 = f32[128]{0:T(128)S(1)} all-reduce(f32[128]{0:T(128)S(1)} %slice.403), channel_id=1, replica_groups=mesh['parts'=2,'warp'=4,'weft'=2,'ply'=2] {'warp','weft','ply'}, use_global_device_ids=true, to_apply=%region_21.22 | all-reduce | flops 128 | bytes 1024 | tf_op jit(solution)/shard_map/psum | solution.py:137
  567.4 29.5 %all-reduce.2 = f32[128]{0:T(128)S(1)} all-reduce(f32[128]{0:T(128)S(1)} %dynamic-update-slice.2), channel_id=1, replica_groups=mesh['parts'=2,'warp'=4,'weft'=2,'ply'=2] {'warp','weft','ply'}, use_global_device_ids=true, to_apply=%add.2 | all-reduce | flops 128 | bytes 1024
  596.8 12.6 %gather_fusion.14 = f32[2048]{0:T(1024)S(1)} fusion(f32[128]{0:T(128)S(1)} %all-reduce.2, s32[2048]{0:T(1024)S(1)} %broadcast_clamp_fusion), kind=kCustom, calls=%fused_computation.14 | custom fusion | bytes 24576 | tf_op jit(solution)/shard_map/gather | solution.py:144
  611.8 8.8 %ragged-dot-none = f32[512,512]{1,0:T(8,128)} custom-call(s32[1]{0:T(128)} %get-tuple-element.27, s32[4]{0:T(128)} %get-tuple-element.28, s32[4]{0:T(128)} %get-tuple-element.29, s32[4]{0:T(128)} %get-tuple-element.30, s32[1]{0:T(128)} %get-tuple-element.27, f32[512,512]{1,0:T(8,128)} %gather_fusion.12, f32[3,512,512]{2,1,0:T(8,128)} %param.16), custom_call_target="tpu_custom_call" | custom-call | flops 268435456 | bytes 5242892 | tf_op jit(solution)/shard_map/ragged_dot_general/ragged-dot-none
  641.1 32.1 %psum.71 = f32[]{:T(128)} all-reduce(f32[]{:T(128)} %fusion.21), channel_id=1, replica_groups=mesh['parts'=2,'warp'=4,'weft'=2,'ply'=2] {'warp','weft','ply'}, use_global_device_ids=true, to_apply=%region_23.24 | all-reduce | flops 1 | bytes 8 | tf_op jit(solution)/shard_map/psum | solution.py:149
  (280 shorter events, 166.1 us)
Async XLA Ops:
  29.4 6.2 collective-permute-start
  32.6 5.1 collective-permute-start.1
  38.5 7.7 %collective-permute-start.2 = (f32[6,1,256]{2,1,0:T(1,128)S(1)}, f32[6,1,256]{2,1,0:T(1,128)S(1)}, u32[]{:S(2)}, u32[]{:S(2)}) collective-permute-start(f32[6,1,256]{2,1,0:T(1,128)S(1)} %get-tuple-element.103), channel_id=1, source_target_pairs={{0,2},{1,3},{4,6},{5,7},{8,10},{9,11},{12,14},{13,15},{16,18},{17,... | collective-permute-start | bytes 18440 | tf_op jit(solution)/shard_map/ppermute | solution.py:17
  41.9 5.5 collective-permute-start.3
  191.2 3.1 collective-permute-start.4
  193.0 3.2 collective-permute-start.5
  196.3 2.8 collective-permute-start.6
  197.6 5.5 collective-permute-start.7
  256.5 3.7 collective-permute-start.8
  257.8 3.2 collective-permute-start.9
  261.1 2.7 collective-permute-start.10
  262.4 5.5 collective-permute-start.11
  408.4 3.1 collective-permute-start.12
  410.2 3.2 collective-permute-start.13
  413.5 2.7 collective-permute-start.14
  414.8 5.5 collective-permute-start.15
  474.6 3.9 collective-permute-start.16
  476.2 3.2 collective-permute-start.17
  479.4 3.7 collective-permute-start.18
  480.7 5.5 collective-permute-start.19
  627.0 3.3 collective-permute-start.20
  628.9 3.2 collective-permute-start.21
  632.1 2.7 collective-permute-start.22
  633.4 5.5 collective-permute-start.23
  (45 other events, 1870.4 us)
where the time goes:
time: 681 us; the launch traced here: 679 us
  blocking collectives  368 us (54%)
  local copies, waits for them, and re-layouts  88.5 us (13%)
  other arithmetic  80.7 us (12%)
  Pallas kernels  53.8 us (8%)
  starting transfers between devices  37 us (5%)
  waiting for transfers between devices  30.1 us (4%)
  matrix products  10.3 us (2%)
  between operations  10.3 us (2%)
    psum x3, blocking collectives, on_device(): lax.psum(jnp.sum(edge_weight * direction * applied), ('warp', 'weft', 'pl...  96.3 us
    psum x3, blocking collectives, on_device(): lax.psum(jnp.sum(edge_weight * residual * precond), ('warp', 'weft', 'ply'))  94.8 us
    psum x3, blocking collectives, on_device(): coarse_rhs = lax.psum(partial_rhs, ('warp', 'weft', 'ply'))  88.5 us
    unnamed x3, blocking collectives  88.4 us
    another operation x6, Pallas kernels  52.5 us
    scatter-add x3, other arithmetic, on_device(): jax.ops.segment_sum(corner_load.reshape(-1), corner_slot.reshape(-1), num...  44 us
    gather x6, local copies, waits for them, and re-layouts, on_device(): corner_vals = jnp.where(corner_live, coarse_sol[corner_pick], 0.0)  37.9 us
    ppermute x12, waiting for transfers between devices, with_halo(): after = lax.ppermute(leading, axis, down)  30.1 us
  transfers between devices with their start and end apart: 24, of which 12 were waited for; matrix products, arithmetic and copies ran while one was open for 1% of the time, Pallas kernels for 0%

commit v1 on v0

--- a/solution.py
+++ b/solution.py
@@ -134,7 +134,9 @@
         partial_rhs = jax.ops.segment_sum(
             corner_load.reshape(-1), corner_slot.reshape(-1), num_segments=coarse_count + 1
         )[:coarse_count]
-        coarse_rhs = lax.psum(partial_rhs, ("warp", "weft", "ply"))
+        coarse_rhs = partial_rhs
+        for name in (("weft", "ply"), "warp"):
+            coarse_rhs = lax.psum(coarse_rhs, name)
         coarse_sol = lax.all_gather(
             jnp.dot(coarse_inv, coarse_rhs, precision=HIGHEST),
             ("warp", "weft", "ply"),

time: 681 us -> 635 us (0.932)
  blocking collectives: 368 us -> 322 us
    psum x3 -> x6, blocking collectives: 88.5 us -> 42.3 us  [on_device(): coarse_rhs = lax.psum(coarse_rhs, name)]
where the time goes in v1:
time: 635 us; the launch traced here: 633 us
  blocking collectives  322 us (51%)
  local copies, waits for them, and re-layouts  88.4 us (14%)
  other arithmetic  80.8 us (13%)
  Pallas kernels  53.7 us (8%)
  starting transfers between devices  37 us (6%)
  waiting for transfers between devices  30.3 us (5%)
  between operations  10.5 us (2%)
  matrix products  10.3 us (2%)
    psum x3, blocking collectives, on_device(): lax.psum(jnp.sum(edge_weight * direction * applied), ('warp', 'weft', 'pl...  96.3 us
    psum x3, blocking collectives, on_device(): lax.psum(jnp.sum(edge_weight * residual * precond), ('warp', 'weft', 'ply'))  94.8 us
    unnamed x3, blocking collectives  88.4 us
    another operation x6, Pallas kernels  52.4 us
    scatter-add x3, other arithmetic, on_device(): jax.ops.segment_sum(corner_load.reshape(-1), corner_slot.reshape(-1), num...  44 us
    psum x6, blocking collectives, on_device(): coarse_rhs = lax.psum(coarse_rhs, name)  42.3 us
    gather x6, local copies, waits for them, and re-layouts, on_device(): corner_vals = jnp.where(corner_live, coarse_sol[corner_pick], 0.0)  37.9 us
    ppermute x12, waiting for transfers between devices, with_halo(): after = lax.ppermute(leading, axis, down)  30.2 us
  transfers between devices with their start and end apart: 24, of which 12 were waited for; matrix products, arithmetic and copies ran while one was open for 1% of the time, Pallas kernels for 0%

profile of v1, /device:TPU:0, one launch (start us, length us, event | category | flops | bytes accessed | tf_op | source)
XLA Modules:
  0.0 632.8 jit_solution(11296015810722087793)
XLA Ops:
  15.8 8.7 %ragged-dot-none.5 = f32[512,512]{1,0:T(8,128)} custom-call(s32[1]{0:T(128)} %get-tuple-element.27, s32[4]{0:T(128)} %get-tuple-element.28, s32[4]{0:T(128)} %get-tuple-element.29, s32[4]{0:T(128)} %get-tuple-element.30, s32[1]{0:T(128)} %get-tuple-element.27, f32[512,512]{1,0:T(8,128)} %gather_fusion, f32[3,512,512]{2,1,0:T(8,128)} %param.17), custom_call_target="tpu_custom_call" | custom-call | flops 268435456 | bytes 5242892 | tf_op jit(solution)/shard_map/ragged_dot_general/ragged-dot-none
  50.5 33.6 %psum.84 = f32[]{:T(128)} all-reduce(f32[]{:T(128)} %multiply_reduce_fusion.2), channel_id=1, replica_groups=mesh['parts'=2,'warp'=4,'weft'=2,'ply'=2] {'warp','weft','ply'}, use_global_device_ids=true, to_apply=%region_4.5 | all-reduce | flops 1 | bytes 8 | tf_op jit(solution)/shard_map/psum | solution.py:128
  87.1 14.7 %scatter_custom_fusion = f32[129]{0:T(256)S(1)} fusion(s32[2048]{0:T(1024)S(1)} %bitcast.138, f32[2048]{0:T(1024)S(1)} %bitcast.142, f32[]{:T(128)} %constant.17.clone.1), kind=kCustom, calls=%fused_computation.187 | custom fusion | flops 2048 | bytes 520 | tf_op jit(solution)/shard_map/scatter-add | solution.py:134
  107.6 8.4 %psum.86 = f32[128]{0:T(128)S(1)} all-reduce(f32[128]{0:T(128)S(1)} %psum.85), channel_id=1, replica_groups=mesh['parts'=2,'warp'=4,'weft'=2,'ply'=2] {'warp'}, use_global_device_ids=true, to_apply=%region_8.9 | all-reduce | flops 128 | bytes 1024 | tf_op jit(solution)/shard_map/psum | solution.py:139
  116.3 29.5 %all-reduce = f32[128]{0:T(128)S(1)} all-reduce(f32[128]{0:T(128)S(1)} %dynamic-update-slice), channel_id=1, replica_groups=mesh['parts'=2,'warp'=4,'weft'=2,'ply'=2] {'warp','weft','ply'}, use_global_device_ids=true, to_apply=%add | all-reduce | flops 128 | bytes 1024
  145.7 12.6 %gather_fusion.4 = f32[2048]{0:T(1024)S(1)} fusion(f32[128]{0:T(128)S(1)} %all-reduce, s32[2048]{0:T(1024)S(1)} %broadcast_clamp_fusion), kind=kCustom, calls=%fused_computation.4 | custom fusion | bytes 24576 | tf_op jit(solution)/shard_map/gather | solution.py:146
  160.7 8.7 %ragged-dot-none.4 = f32[512,512]{1,0:T(8,128)} custom-call(s32[1]{0:T(128)} %get-tuple-element.27, s32[4]{0:T(128)} %get-tuple-element.28, s32[4]{0:T(128)} %get-tuple-element.29, s32[4]{0:T(128)} %get-tuple-element.30, s32[1]{0:T(128)} %get-tuple-element.27, f32[512,512]{1,0:T(8,128)} %gather_fusion.2, f32[3,512,512]{2,1,0:T(8,128)} %param.16), custom_call_target="tpu_custom_call" | custom-call | flops 268435456 | bytes 5242892 | tf_op jit(solution)/shard_map/ragged_dot_general/ragged-dot-none
  189.7 32.0 %psum.87 = f32[]{:T(128)} all-reduce(f32[]{:T(128)} %fusion.23), channel_id=1, replica_groups=mesh['parts'=2,'warp'=4,'weft'=2,'ply'=2] {'warp','weft','ply'}, use_global_device_ids=true, to_apply=%region_10.11 | all-reduce | flops 1 | bytes 8 | tf_op jit(solution)/shard_map/psum | solution.py:151
  227.0 8.7 %ragged-dot-none.3 = f32[512,512]{1,0:T(8,128)} custom-call(s32[1]{0:T(128)} %get-tuple-element.27, s32[4]{0:T(128)} %get-tuple-element.28, s32[4]{0:T(128)} %get-tuple-element.29, s32[4]{0:T(128)} %get-tuple-element.30, s32[1]{0:T(128)} %get-tuple-element.27, f32[512,512]{1,0:T(8,128)} %gather_fusion.5, f32[3,512,512]{2,1,0:T(8,128)} %param.17), custom_call_target="tpu_custom_call" | custom-call | flops 268435456 | bytes 5242892 | tf_op jit(solution)/shard_map/ragged_dot_general/ragged-dot-none
  254.6 30.7 %psum.88 = f32[]{:T(128)} all-reduce(f32[]{:T(128)} %multiply_reduce_fusion.1), channel_id=1, replica_groups=mesh['parts'=2,'warp'=4,'weft'=2,'ply'=2] {'warp','weft','ply'}, use_global_device_ids=true, to_apply=%region_12.13 | all-reduce | flops 1 | bytes 8 | tf_op jit(solution)/shard_map/psum | solution.py:128
  289.1 14.7 %scatter_custom_fusion.1 = f32[129]{0:T(256)S(1)} fusion(s32[2048]{0:T(1024)S(1)} %bitcast.139, f32[2048]{0:T(1024)S(1)} %bitcast.143, f32[]{:T(128)} %constant.17.clone.1), kind=kCustom, calls=%fused_computation.185 | custom fusion | flops 2048 | bytes 520 | tf_op jit(solution)/shard_map/scatter-add | solution.py:134
  309.5 8.4 %psum.90 = f32[128]{0:T(128)S(1)} all-reduce(f32[128]{0:T(128)S(1)} %psum.89), channel_id=1, replica_groups=mesh['parts'=2,'warp'=4,'weft'=2,'ply'=2] {'warp'}, use_global_device_ids=true, to_apply=%region_16.17 | all-reduce | flops 128 | bytes 1024 | tf_op jit(solution)/shard_map/psum | solution.py:139
  318.2 29.5 %all-reduce.1 = f32[128]{0:T(128)S(1)} all-reduce(f32[128]{0:T(128)S(1)} %dynamic-update-slice.1), channel_id=1, replica_groups=mesh['parts'=2,'warp'=4,'weft'=2,'ply'=2] {'warp','weft','ply'}, use_global_device_ids=true, to_apply=%add.1 | all-reduce | flops 128 | bytes 1024
  347.7 12.6 %gather_fusion.9 = f32[2048]{0:T(1024)S(1)} fusion(f32[128]{0:T(128)S(1)} %all-reduce.1, s32[2048]{0:T(1024)S(1)} %broadcast_clamp_fusion), kind=kCustom, calls=%fused_computation.9 | custom fusion | bytes 24576 | tf_op jit(solution)/shard_map/gather | solution.py:146
  362.6 8.7 %ragged-dot-none.2 = f32[512,512]{1,0:T(8,128)} custom-call(s32[1]{0:T(128)} %get-tuple-element.27, s32[4]{0:T(128)} %get-tuple-element.28, s32[4]{0:T(128)} %get-tuple-element.29, s32[4]{0:T(128)} %get-tuple-element.30, s32[1]{0:T(128)} %get-tuple-element.27, f32[512,512]{1,0:T(8,128)} %gather_fusion.7, f32[3,512,512]{2,1,0:T(8,128)} %param.16), custom_call_target="tpu_custom_call" | custom-call | flops 268435456 | bytes 5242892 | tf_op jit(solution)/shard_map/ragged_dot_general/ragged-dot-none
  391.6 32.2 %psum.91 = f32[]{:T(128)} all-reduce(f32[]{:T(128)} %fusion.22), channel_id=1, replica_groups=mesh['parts'=2,'warp'=4,'weft'=2,'ply'=2] {'warp','weft','ply'}, use_global_device_ids=true, to_apply=%region_18.19 | all-reduce | flops 1 | bytes 8 | tf_op jit(solution)/shard_map/psum | solution.py:151
  430.9 8.7 %ragged-dot-none.1 = f32[512,512]{1,0:T(8,128)} custom-call(s32[1]{0:T(128)} %get-tuple-element.27, s32[4]{0:T(128)} %get-tuple-element.28, s32[4]{0:T(128)} %get-tuple-element.29, s32[4]{0:T(128)} %get-tuple-element.30, s32[1]{0:T(128)} %get-tuple-element.27, f32[512,512]{1,0:T(8,128)} %gather_fusion.10, f32[3,512,512]{2,1,0:T(8,128)} %param.17), custom_call_target="tpu_custom_call" | custom-call | flops 268435456 | bytes 5242892 | tf_op jit(solution)/shard_map/ragged_dot_general/ragged-dot-none
  457.7 30.6 %psum.92 = f32[]{:T(128)} all-reduce(f32[]{:T(128)} %multiply_reduce_fusion), channel_id=1, replica_groups=mesh['parts'=2,'warp'=4,'weft'=2,'ply'=2] {'warp','weft','ply'}, use_global_device_ids=true, to_apply=%region_20.21 | all-reduce | flops 1 | bytes 8 | tf_op jit(solution)/shard_map/psum | solution.py:128
  492.4 14.7 %scatter_custom_fusion.2 = f32[129]{0:T(256)S(1)} fusion(s32[2048]{0:T(1024)S(1)} %bitcast.140, f32[2048]{0:T(1024)S(1)} %bitcast.141, f32[]{:T(128)} %constant.17.clone.1), kind=kCustom, calls=%fused_computation.183 | custom fusion | flops 2048 | bytes 520 | tf_op jit(solution)/shard_map/scatter-add | solution.py:134
  512.8 8.4 %psum.94 = f32[128]{0:T(128)S(1)} all-reduce(f32[128]{0:T(128)S(1)} %psum.93), channel_id=1, replica_groups=mesh['parts'=2,'warp'=4,'weft'=2,'ply'=2] {'warp'}, use_global_device_ids=true, to_apply=%region_24.25 | all-reduce | flops 128 | bytes 1024 | tf_op jit(solution)/shard_map/psum | solution.py:139
  521.5 29.5 %all-reduce.2 = f32[128]{0:T(128)S(1)} all-reduce(f32[128]{0:T(128)S(1)} %dynamic-update-slice.2), channel_id=1, replica_groups=mesh['parts'=2,'warp'=4,'weft'=2,'ply'=2] {'warp','weft','ply'}, use_global_device_ids=true, to_apply=%add.2 | all-reduce | flops 128 | bytes 1024
  551.0 12.6 %gather_fusion.14 = f32[2048]{0:T(1024)S(1)} fusion(f32[128]{0:T(128)S(1)} %all-reduce.2, s32[2048]{0:T(1024)S(1)} %broadcast_clamp_fusion), kind=kCustom, calls=%fused_computation.14 | custom fusion | bytes 24576 | tf_op jit(solution)/shard_map/gather | solution.py:146
  565.9 8.7 %ragged-dot-none = f32[512,512]{1,0:T(8,128)} custom-call(s32[1]{0:T(128)} %get-tuple-element.27, s32[4]{0:T(128)} %get-tuple-element.28, s32[4]{0:T(128)} %get-tuple-element.29, s32[4]{0:T(128)} %get-tuple-element.30, s32[1]{0:T(128)} %get-tuple-element.27, f32[512,512]{1,0:T(8,128)} %gather_fusion.12, f32[3,512,512]{2,1,0:T(8,128)} %param.16), custom_call_target="tpu_custom_call" | custom-call | flops 268435456 | bytes 5242892 | tf_op jit(solution)/shard_map/ragged_dot_general/ragged-dot-none
  595.2 32.1 %psum.95 = f32[]{:T(128)} all-reduce(f32[]{:T(128)} %fusion.21), channel_id=1, replica_groups=mesh['parts'=2,'warp'=4,'weft'=2,'ply'=2] {'warp','weft','ply'}, use_global_device_ids=true, to_apply=%region_26.27 | all-reduce | flops 1 | bytes 8 | tf_op jit(solution)/shard_map/psum | solution.py:151
  (283 shorter events, 183.5 us)
Async XLA Ops:
  29.4 6.1 collective-permute-start
  32.5 5.1 collective-permute-start.1
  38.5 7.6 %collective-permute-start.2 = (f32[6,1,256]{2,1,0:T(1,128)S(1)}, f32[6,1,256]{2,1,0:T(1,128)S(1)}, u32[]{:S(2)}, u32[]{:S(2)}) collective-permute-start(f32[6,1,256]{2,1,0:T(1,128)S(1)} %get-tuple-element.103), channel_id=1, source_target_pairs={{0,2},{1,3},{4,6},{5,7},{8,10},{9,11},{12,14},{13,15},{16,18},{17,... | collective-permute-start | bytes 18440 | tf_op jit(solution)/shard_map/ppermute | solution.py:17
  41.9 5.5 collective-permute-start.3
  175.8 3.1 collective-permute-start.4
  177.6 3.2 collective-permute-start.5
  180.9 2.8 collective-permute-start.6
  182.2 5.5 collective-permute-start.7
  241.2 3.7 collective-permute-start.8
  242.5 3.2 collective-permute-start.9
  245.7 2.7 collective-permute-start.10
  247.0 5.5 collective-permute-start.11
  377.8 3.1 collective-permute-start.12
  379.5 3.2 collective-permute-start.13
  382.8 2.7 collective-permute-start.14
  384.1 5.5 collective-permute-start.15
  443.9 3.9 collective-permute-start.16
  445.5 3.2 collective-permute-start.17
  448.8 3.7 collective-permute-start.18
  450.1 5.5 collective-permute-start.19
  581.1 3.3 collective-permute-start.20
  583.0 3.2 collective-permute-start.21
  586.3 2.7 collective-permute-start.22
  587.5 5.5 collective-permute-start.23
  (45 other events, 1747.9 us)
